TPU v7x, 32 devices: a whole 2x2x4 slice. The times are simulated.
32 devices in a mesh: band: 2 (over x), row: 16 (over z, y, core).
Axes of the slice: x: 2, y: 2, z: 4, core: 2. Of those that a mesh axis runs over, the one named last changes fastest.
Arguments:
- tiles: bfloat16 [256, 96, 64, 128], P(('band', 'row')), parts along dimension 0, may hold values from -0.0390625 to 0.0390625
- tile_light: int32 [256, 96], P(('band', 'row')), parts along dimension 0, may hold values from 0 to 255
- tile_count: int32 [256], P(('band', 'row')), parts along dimension 0, may hold values from 24 to 96, as said below
- env_maps: bfloat16 [16384, 384], P('row'), may hold values from 0.099609375 to 10
- frame_slot: int32 [128], replicated, may hold values from 0 to 127, each once
Outputs:
- frames: bfloat16 [128, 32768], P('row', 'band'), parts along dimension 1
There are 2 independent parts, one for each index of `band`. A program takes and returns all parts, laid end to end along the dimension named above; an argument that names none is the same for every part. Nothing has to cross between parts.
Inputs may be any that keep to these rules, and one draw needn't show every extreme that they name: `tile_count`: every block has at least a quarter of the slots used, and some block uses all 96.
All inputs are finite; a program needn't handle non-finite values.
Results may differ from a plain program's by a relative error of at most 0.001.
Values may be sent and summed in bfloat16 or wider, within the bound.
A program may use at most 128 MiB of HBM per device.

v0:
```python
import jax
import jax.numpy as jnp
from jax import lax
from jax.sharding import PartitionSpec as P

F = 128
CHANNELS = 3


def body(tiles, tile_light, tile_count, env_maps, frame_slot):
    blocks_dev, slots, depth, width = tiles.shape
    own_channel = lax.axis_index("row") % CHANNELS
    gathered = lax.all_gather(env_maps, "row", axis=0, tiled=True)
    whole = gathered.reshape(gathered.shape[0], CHANNELS, F)
    channel_map = lax.dynamic_index_in_dim(whole, own_channel, 1, keepdims=False)
    blocks = channel_map.reshape(channel_map.shape[0] // 64, 64, F)
    chosen = blocks[tile_light]
    active = (jnp.arange(slots, dtype=jnp.int32)[None, :] < tile_count[:, None]).astype(
        jnp.bfloat16
    )
    chosen = chosen * active[:, :, None, None]
    relit_image = jnp.einsum(
        "gslr,gslf->fgr", tiles, chosen, preferred_element_type=jnp.float32
    ).astype(jnp.bfloat16)
    relit_image = relit_image[frame_slot]
    relit_image = relit_image.reshape(F, blocks_dev * width)
    return lax.all_to_all(relit_image, "row", split_axis=0, concat_axis=1, tiled=True)


def solution(mesh):
    return jax.shard_map(
        body,
        mesh=mesh,
        in_specs=(
            P(("band", "row"), None, None, None),
            P(("band", "row"), None),
            P(("band", "row")),
            P("row", None),
            P(),
        ),
        out_specs=P("row", "band"),
        check_vma=False,
    )
```

profile of v0, /device:TPU:0, one launch (start us, length us, event | category | flops | bytes accessed | tf_op | source)
XLA Modules:
  0.0 177.8 jit_solution(10025991901678338919)
XLA Ops:
  6.5 0.0 all-gather.2.cloned.1.call-start
  6.5 2.3 %copy.7 = bf16[1024,384]{0,1:T(8,128)(2,1)} copy(bf16[1024,384]{1,0:T(8,128)(2,1)} %param.8) | data formatting | bytes 1572864 | tf_op args[3]
  8.9 0.0 all-gather.2.cloned.1.call-update
  8.9 0.7 compare_select_fusion
  9.6 0.1 reshape.38
  9.7 0.7 compare_select_fusion.1
  10.4 0.7 fusion.12
  11.1 102.0 %all-gather.2.cloned.1.call-done = bf16[16384,384]{0,1:T(8,128)(2,1)} async-done(((bf16[1024,384]{0,1:T(8,128)(2,1)}), bf16[16384,384]{0,1:T(8,128)(2,1)}) %all-gather.2.cloned.1.call-update) | async-done | bytes 12582928 | tf_op jit(solution)/shard_map/all_gather | solution.py:13
  113.1 4.5 %constant_dynamic-slice_fusion = bf16[16384,1,128]{0,2,1:T(8,128)(2,1)} fusion(bf16[16384,3,128]{0,2,1:T(8,128)(2,1)} %bitcast.18, s32[]{:T(128)S(6)} %select_n.18), kind=kLoop, calls=%fused_computation.14 | loop fusion | bytes 8388612 | tf_op jit(solution)/shard_map/jit(dynamic_index_in_dim)/dynamic_slice | solution.py:15
  117.6 6.4 %copy.8 = bf16[16384,1,128]{2,0,1:T(8,128)(2,1)} copy(bf16[16384,1,128]{0,2,1:T(8,128)(2,1)} %constant_dynamic-slice_fusion) | data formatting | bytes 8388608 | tf_op jit(solution)/shard_map/jit(dynamic_index_in_dim)/dynamic_slice | solution.py:15
  124.0 21.8 %gather_fusion = bf16[768,64,128]{2,1,0:T(8,128)(2,1)} fusion(bf16[256,64,128]{2,1,0:T(8,128)(2,1)} %bitcast.16, s32[1024]{0:T(1024)S(1)} %pad_clamp_fusion.1), kind=kCustom, calls=%fused_computation | custom fusion | bytes 25168896 | tf_op jit(solution)/shard_map/gather | solution.py:17
  145.8 10.7 %fusion.9 = bf16[128,8,128]{2,0,1:T(8,128)(2,1)S(1)} fusion(bf16[8,96,64,128]{3,2,1,0:T(8,128)(2,1)} %param.5, bf16[8,96,64,128]{3,2,1,0:T(8,128)(2,1)} %bitcast.17, bf16[8,96]{1,0:T(8,128)(2,1)S(1)} %fusion.12), kind=kOutput, calls=%fused_computation.7 | convolution fusion | flops 1617035264 | bytes 25429504 | tf_op jit(solution)/shard_map/gslr,gslf->fgr/dot_general | solution.py:22
  156.5 0.2 copy.11
  156.7 0.7 gather_fusion.1
  157.4 0.1 all_to_all.14
  157.5 12.7 %all_to_all.19 = bf16[16,8,1024]{2,1,0:T(8,128)(2,1)S(1)} all-to-all(bf16[16,8,1024]{2,1,0:T(8,128)(2,1)S(1)} %all_to_all.14), channel_id=1, replica_groups=mesh['band'=2,'row'=16] {'row'}, dimensions={0} | all-to-all | bytes 524288 | tf_op jit(solution)/shard_map/all_to_all | solution.py:27
  170.3 0.7 copy.16
  (2 shorter events, 0.0 us)
Async XLA Ops:
  6.5 106.5 %all-gather.2.cloned.1.call-start = ((), (), s32[]{:S(2)}) async-start(), calls=%async_computation.1 | async-start | bytes 13369344 | tf_op jit(solution)/shard_map/all_gather | solution.py:13
Sparse Core Ops, SparseCore 0:
  9.5 103.4 all-gather.1
where the time goes:
time: 178 us
  waiting for transfers between devices  102 us (57%)
  local copies, waits for them, and re-layouts  36.8 us (21%)
  between operations  13.4 us (8%)
  blocking collectives  12.7 us (7%)
  matrix products  10.7 us (6%)
  other arithmetic  2.09 us (1%)
    all_gather x1, waiting for transfers between devices, body(): gathered = lax.all_gather(env_maps, 'row', axis=0, tiled=True)  102 us
    gather x1, local copies, waits for them, and re-layouts, body(): chosen = blocks[tile_light]  21.8 us
    all_to_all x1, blocking collectives, body(): lax.all_to_all(relit_image, 'row', split_axis=0, concat_axis=1, tiled=True)  12.7 us
    dynamic_slice x2, local copies, waits for them, and re-layouts, body(): lax.dynamic_index_in_dim(whole, own_channel, 1, keepdims=False)  10.9 us
    dot_general x1, matrix products, body(): jnp.einsum('gslr,gslf->fgr', tiles, chosen, preferred_element_type=jnp.fl...  10.7 us
  transfers between devices with their start and end apart: 1, of which 1 were waited for; matrix products, arithmetic and copies ran while one was open for 1% of the time, Pallas kernels for 0%

commit v1 on v0

v1 whole, which is shorter than its diff:
```python
import functools
import jax
import jax.numpy as jnp
from jax import lax
from jax.experimental import pallas as pl
from jax.experimental.pallas import tpu as pltpu
from jax.sharding import PartitionSpec as P

F = 128
CHANNELS = 3
DEPTH = 64
J = 4
JC = 2
MESH = pl.DeviceIdType.MESH


def kernel(Z, W, light, count, slot, env, tiles, out,
           own, trunk, emap, dup, tv, sb, zs, zr, fs, fr, xs, xr, ts, os_, or_):
    R = 4 * Z
    G, slots = light.shape
    L = env.shape[0]
    KJ = F // J
    KC = F // JC
    fpd = F // R
    X = L - W
    x = lax.axis_index("band")
    row = lax.axis_index("row")
    core = lax.rem(row, 2)
    y = lax.rem(lax.div(row, 2), 2)
    z = lax.div(row, 4)
    me4 = y * 2 + core
    mych = lax.rem(row, CHANNELS)
    off = pl.multiple_of(x * X, 128)
    xoff = pl.multiple_of(x * W, 128)
    xland = pl.multiple_of((1 - x) * W, 128)

    barrier = pltpu.get_barrier_semaphore()

    def greet(i, _):
        pl.semaphore_signal(barrier, inc=1, device_id=(x, lax.rem(row + i, R)), device_id_type=MESH)
        return 0

    lax.fori_loop(1, R, greet, 0)
    pl.semaphore_signal(barrier, inc=1, device_id=(1 - x, row), device_id_type=MESH)

    def tile_copy(g):
        return pltpu.make_async_copy(tiles.at[g], tv.at[g], ts.at[g])

    perm = (slot[...] == lax.broadcasted_iota(jnp.int32, (F, F), 1)).astype(jnp.float32).astype(jnp.bfloat16)
    for c in range(CHANNELS):
        own[c] = lax.dot_general(perm, env[:, c * F:(c + 1) * F], (((1,), (1,)), ((), ())),
                                 preferred_element_type=jnp.float32).astype(jnp.bfloat16)
    for jc in range(JC):
        dup[jc, dup.shape[1] - 1] = jnp.zeros((KC, 128), jnp.bfloat16)

    pl.semaphore_wait(barrier, R)

    def rows_of(j):
        return pl.ds(pl.multiple_of(j * KJ, KJ), KJ)

    def z_copy(j, zz, up, mine):
        rows = rows_of(j)
        src = own.at[:, rows, pl.ds(off, W)] if mine else trunk.at[zz, :, rows, :]
        to = row + 4 if up else row - 4
        return pltpu.make_async_remote_copy(
            src_ref=src, dst_ref=trunk.at[zz, :, rows, :],
            send_sem=zs.at[j, 0 if up else 1, zz], recv_sem=zr.at[j, zz],
            device_id=(x, to), device_id_type=MESH)

    def z_wait(j, zz):
        here = trunk.at[zz, :, rows_of(j), :]
        pltpu.make_async_remote_copy(
            src_ref=here, dst_ref=here, send_sem=zs.at[j, 0, zz], recv_sem=zr.at[j, zz],
            device_id=(x, row), device_id_type=MESH).wait_recv()

    def peer(k):
        y2 = 1 - y if k // 2 else y
        c2 = 1 - core if k % 2 else core
        return y2, c2

    def fan_copy(j, zz, k, mine):
        y2, c2 = peer(k)
        to = (z * 2 + y2) * 2 + c2
        ch = lax.rem(to, CHANNELS)
        rows = rows_of(j)
        if mine:
            src, dst = own.at[ch, rows, :], emap.at[zz, me4, rows, :]
        else:
            src, dst = trunk.at[zz, ch, rows, :], emap.at[zz, me4, rows, pl.ds(off, W)]
        if k == 0:
            return pltpu.make_async_copy(src, dst, fr.at[j, zz, me4])
        return pltpu.make_async_remote_copy(
            src_ref=src, dst_ref=dst, send_sem=fs.at[j, zz, k], recv_sem=fr.at[j, zz, me4],
            device_id=(x, to), device_id_type=MESH)

    def fan_wait(j, zz, k, mine):
        if k == 0:
            fan_copy(j, zz, 0, mine).wait()
            return
        y2, c2 = peer(k)
        src4 = y2 * 2 + c2
        rows = rows_of(j)
        here = emap.at[zz, src4, rows, :] if mine else emap.at[zz, src4, rows, pl.ds(off, W)]
        pltpu.make_async_remote_copy(
            src_ref=here, dst_ref=here, send_sem=fs.at[j, zz, k], recv_sem=fr.at[j, zz, src4],
            device_id=(x, row), device_id_type=MESH).wait_recv()

    def x_copy(j, zz, at):
        here = emap.at[zz, :, rows_of(j), pl.ds(at, X)]
        return pltpu.make_async_remote_copy(
            src_ref=here, dst_ref=here, send_sem=xs.at[j, zz], recv_sem=xr.at[j, zz],
            device_id=(1 - x, row), device_id_type=MESH)

    def each_block(t, own_fn, other_fn):
        @pl.when(t == 0)
        def _():
            own_fn()

        @pl.when((t > 0) & (z - t >= 0))
        def _():
            other_fn(z - t, True)

        @pl.when((t > 0) & (z + t < Z))
        def _():
            other_fn(z + t, False)

    def can_go(up):
        return z < Z - 1 if up else z > 0

    def stage_a(j, t):
        def mine():
            for up in (True, False):
                @pl.when(can_go(up))
                def _():
                    z_copy(j, z, up, True).start()
            for k in (2, 3, 1, 0):
                fan_copy(j, z, k, True).start()

        def other(zz, up):
            z_wait(j, zz)

            @pl.when(can_go(up))
            def _():
                z_copy(j, zz, up, False).start()
            for k in (2, 3, 1, 0):
                fan_copy(j, zz, k, False).start()

        each_block(t, mine, other)

    def stage_b(j, t):
        def mine():
            for k in range(4):
                fan_wait(j, z, k, True)

        def other(zz, up):
            for k in range(4):
                fan_wait(j, zz, k, False)
            x_copy(j, zz, xoff).start()

        each_block(t, mine, other)

    low = lax.broadcasted_iota(jnp.int32, (KJ, 128), 1) < DEPTH

    def build(j, zz):
        jc = lax.div(j, J // JC)
        krows = pl.ds(pl.multiple_of(lax.rem(j, J // JC) * KJ, KJ), KJ)
        per = L // DEPTH

        def shard(s, _):
            for c in range(L // 128):
                a = emap[zz, s, rows_of(j), c * 128:(c + 1) * 128]
                b = pltpu.roll(a, DEPTH, 1)
                at = (zz * 4 + s) * per + 2 * c
                dup[jc, at, krows, :] = jnp.where(low, a, b)
                dup[jc, at + 1, krows, :] = jnp.where(low, b, a)
            return 0

        lax.fori_loop(0, 4, shard, 0)

    def stage_c(j, t):
        def mine():
            build(j, z)

        def other(zz, up):
            x_copy(j, zz, xland).wait_recv()
            build(j, zz)

        each_block(t, mine, other)

    N = J * Z

    def step(n):
        for lag, stage in ((0, stage_a), (1, stage_b), (2, stage_c)):
            m = n - lag

            @pl.when((m >= 0) & (m < N))
            def _(m=m, stage=stage):
                stage(lax.div(m, Z), lax.rem(m, Z))

    zero = dup.shape[1] - 1
    SL = 16
    lowc = lax.broadcasted_iota(jnp.int32, (KC, 128), 1) < DEPTH

    def multiply(jc, gp):
        def one(g):
            used = count[g]

            def some(q, acc):
                parts = []
                for p in range(SL // 2):
                    s = q * SL + 2 * p
                    i0 = jnp.where(s < used, light[g, s], zero)
                    i1 = jnp.where(s + 1 < used, light[g, s + 1], zero)
                    parts.append(jnp.where(lowc, dup[jc, i0], dup[jc, i1]))
                lhs = jnp.concatenate(parts, axis=1)
                rhs = tv[g, pl.ds(pl.multiple_of(q * SL * DEPTH, SL * DEPTH), SL * DEPTH), :]
                return acc + jnp.dot(lhs, rhs, preferred_element_type=jnp.float32)

            return lax.fori_loop(0, slots // SL, some, jnp.zeros((KC, 128), jnp.float32))

        a, b = one(2 * gp), one(2 * gp + 1)
        rows = pl.ds(pl.multiple_of(gp * 2 * fpd, 2 * fpd), 2 * fpd)
        for i in range(R // JC):
            both = jnp.concatenate([a[i * fpd:(i + 1) * fpd], b[i * fpd:(i + 1) * fpd]], axis=0)
            sb[jc * (R // JC) + i, rows, :] = both.astype(jnp.bfloat16)

    def out_copy(d):
        return pltpu.make_async_remote_copy(
            src_ref=sb.at[d], dst_ref=out.at[row], send_sem=os_.at[d], recv_sem=or_.at[row],
            device_id=(x, d), device_id_type=MESH)

    def out_local():
        return pltpu.make_async_copy(sb.at[row], out.at[row], or_.at[row])

    def send(jc):
        def one(i, _):
            d = jc * (R // JC) + lax.rem(row + i, R // JC)

            @pl.when(d != row)
            def _():
                out_copy(d).start()

            @pl.when(d == row)
            def _():
                out_local().start()
            return 0

        lax.fori_loop(0, R // JC, one, 0)

    GP = G // 2
    first = N // JC + 2
    rest = N + 2 - first
    per = max(1, rest // GP)

    for g in range(G):
        tile_copy(g).start()
    lax.fori_loop(0, first, lambda n, _: (step(n), 0)[1], 0)
    for g in range(G):
        tile_copy(g).wait()

    def second(i, _):
        step(first + i)

        @pl.when((lax.rem(i, per) == 0) & (lax.div(i, per) < GP))
        def _():
            multiply(0, lax.div(i, per))

        @pl.when(i == (GP - 1) * per)
        def _():
            send(0)
        return 0

    lax.fori_loop(0, rest, second, 0)
    lax.fori_loop(0, GP, lambda gp, _: (multiply(1, gp), 0)[1], 0)
    send(1)

    def drain(n, _):
        j, t = lax.div(n, Z), lax.rem(n, Z)

        def mine():
            for up in (True, False):
                @pl.when(can_go(up))
                def _():
                    z_copy(j, z, up, True).wait_send()
            for k in (1, 2, 3):
                fan_copy(j, z, k, True).wait_send()

        def other(zz, up):
            @pl.when(can_go(up))
            def _():
                z_copy(j, zz, up, False).wait_send()
            for k in (1, 2, 3):
                fan_copy(j, zz, k, False).wait_send()
            x_copy(j, zz, xoff).wait_send()

        each_block(t, mine, other)
        return 0

    lax.fori_loop(0, N, drain, 0)

    def finish(d, _):
        @pl.when(d != row)
        def _():
            out_copy(d).wait_send()
            pltpu.make_async_remote_copy(
                src_ref=out.at[d], dst_ref=out.at[d], send_sem=os_.at[d], recv_sem=or_.at[d],
                device_id=(x, d), device_id_type=MESH).wait_recv()

        @pl.when(d == row)
        def _():
            out_local().wait()
        return 0

    lax.fori_loop(0, R, finish, 0)


def fused(Z, W, tiles, tile_light, tile_count, env_maps, frame_slot):
    R = 4 * Z
    G, slots, depth, width = tiles.shape
    L = env_maps.shape[0]
    fpd = F // R
    bf = jnp.bfloat16
    dma = pltpu.SemaphoreType.DMA
    vmem = pl.BlockSpec(memory_space=pltpu.VMEM)
    smem = pl.BlockSpec(memory_space=pltpu.SMEM)
    pieces = pl.pallas_call(
        functools.partial(kernel, Z, W),
        out_shape=jax.ShapeDtypeStruct((R, G * fpd, width), bf),
        in_specs=[smem, smem, vmem, vmem, pl.BlockSpec(memory_space=pl.ANY)],
        out_specs=vmem,
        scratch_shapes=[
            pltpu.VMEM((CHANNELS, F, L), bf),
            pltpu.VMEM((Z, CHANNELS, F, W), bf),
            pltpu.VMEM((Z, 4, F, L), bf),
            pltpu.VMEM((JC, R * L // DEPTH + 1, F // JC, 128), bf),
            pltpu.VMEM((G, slots * depth, width), bf),
            pltpu.VMEM((R, G * fpd, width), bf),
            dma((J, 2, Z)), dma((J, Z)), dma((J, Z, 4)), dma((J, Z, 4)),
            dma((J, Z)), dma((J, Z)), dma((G,)), dma((R,)), dma((R,)),
        ],
        compiler_params=pltpu.CompilerParams(
            collective_id=0, has_side_effects=True, vmem_limit_bytes=56 * 1024 * 1024),
    )(tile_light, tile_count, frame_slot.reshape(F, 1), env_maps,
      tiles.reshape(G, slots * depth, width))
    return pieces.reshape(R, G, fpd, width).transpose(2, 0, 1, 3).reshape(fpd, R * G * width)


def plain(tiles, tile_light, tile_count, env_maps, frame_slot):
    blocks_dev, slots, depth, width = tiles.shape
    own_channel = lax.axis_index("row") % CHANNELS
    gathered = lax.all_gather(env_maps, "row", axis=0, tiled=True)
    whole = gathered.reshape(gathered.shape[0], CHANNELS, F)
    channel_map = lax.dynamic_index_in_dim(whole, own_channel, 1, keepdims=False)
    blocks = channel_map.reshape(channel_map.shape[0] // depth, depth, F)
    chosen = blocks[tile_light]
    active = (jnp.arange(slots, dtype=jnp.int32)[None, :] < tile_count[:, None]).astype(jnp.bfloat16)
    chosen = chosen * active[:, :, None, None]
    relit = jnp.einsum("gslr,gslf->fgr", tiles, chosen,
                       preferred_element_type=jnp.float32).astype(jnp.bfloat16)
    relit = relit[frame_slot].reshape(F, blocks_dev * width)
    return lax.all_to_all(relit, "row", split_axis=0, concat_axis=1, tiled=True)


def solution(mesh):
    rows, bands = mesh.shape["row"], mesh.shape["band"]

    def body(tiles, tile_light, tile_count, env_maps, frame_slot):
        L = env_maps.shape[0]
        fits = bands == 2 and rows % 8 == 0 and (F // rows) % 8 == 0 and L % 1024 == 0
        if not fits:
            return plain(tiles, tile_light, tile_count, env_maps, frame_slot)
        return fused(rows // 4, L * 5 // 8, tiles, tile_light, tile_count, env_maps, frame_slot)

    return jax.shard_map(
        body,
        mesh=mesh,
        in_specs=(
            P(("band", "row"), None, None, None),
            P(("band", "row"), None),
            P(("band", "row")),
            P("row", None),
            P(),
        ),
        out_specs=P("row", "band"),
        check_vma=False,
    )
```

time: 178 us -> 92.9 us (0.52)
  the two profiles are of different devices: /device:TPU:0 before, /device:TPU:25 now
where the time goes in v1:
time: 92.9 us; the launch traced here: 92.7 us
  Pallas kernels  89.6 us (96%)
  local copies, waits for them, and re-layouts  3.06 us (3%)
    pallas_call x1, Pallas kernels, fused(): pl.pallas_call(functools.partial(kernel, Z, W), out_shape=jax.ShapeDtypeS...  89.6 us

profile of v1, /device:TPU:25, one launch (start us, length us, event | category | flops | bytes accessed | tf_op | source)
XLA Modules:
  0.0 92.7 jit_solution(6409486909608605458)
XLA Ops:
  0.0 1.4 %copy.6.slot = s32[128,1]{1,0:T(8,128)} copy(s32[128,1]{0,1:T(1,128)} %bitcast.9) | data formatting | bytes 1024 | tf_op jit(solution)/shard_map/reshape | solution.py:343
  1.4 89.6 %shard_map.55 = bf16[16,64,128]{2,1,0:T(8,128)(2,1)} custom-call(s32[8,96]{1,0:T(8,128)} %light.1, s32[8]{0:T(128)} %count.1, s32[128,1]{1,0:T(8,128)} %copy.6.slot, bf16[1024,384]{1,0:T(8,128)(2,1)} %env.1, bf16[8,6144,128]{2,1,0:T(8,128)(2,1)} %bitcast.7), custom_call_target="tpu_custom_call" | custom-call | tf_op jit(solution)/shard_map/pallas_call | solution.py:326
  91.0 1.7 %copy.8 = bf16[8,16384]{1,0:T(8,128)(2,1)} copy(bf16[8,16384]{1,0:T(8,128)(2,1)} %bitcast.8) | data formatting | bytes 524288

commit v2 on v1

--- a/solution.py
+++ b/solution.py
@@ -11,6 +11,9 @@
 DEPTH = 64
 J = 4
 JC = 2
+SUB = J // JC
+LAG_B = 1
+LAG_C = 3
 MESH = pl.DeviceIdType.MESH
 
 
@@ -127,12 +130,14 @@
     def can_go(up):
         return z < Z - 1 if up else z > 0
 
+    def own_out(j):
+        for up in (True, False):
+            @pl.when(can_go(up))
+            def _():
+                z_copy(j, z, up, True).start()
+
     def stage_a(j, t):
         def mine():
-            for up in (True, False):
-                @pl.when(can_go(up))
-                def _():
-                    z_copy(j, z, up, True).start()
             for k in (2, 3, 1, 0):
                 fan_copy(j, z, k, True).start()
 
@@ -146,6 +151,10 @@
                 fan_copy(j, zz, k, False).start()
 
         each_block(t, mine, other)
+
+        @pl.when((t == max(Z - 2, 0)) & (lax.rem(j, SUB) == SUB - 1) & (j < J - 1))
+        def _():
+            lax.fori_loop(0, SUB, lambda i, _: (own_out(j + 1 + i), 0)[1], 0)
 
     def stage_b(j, t):
         def mine():
@@ -190,22 +199,24 @@
     N = J * Z
 
     def step(n):
-        for lag, stage in ((0, stage_a), (1, stage_b), (2, stage_c)):
+        for lag, stage in ((0, stage_a), (LAG_B, stage_b), (LAG_C, stage_c)):
             m = n - lag
 
             @pl.when((m >= 0) & (m < N))
             def _(m=m, stage=stage):
-                stage(lax.div(m, Z), lax.rem(m, Z))
+                stage(lax.div(m, SUB * Z) * SUB + lax.rem(m, SUB), lax.rem(lax.div(m, SUB), Z))
 
     zero = dup.shape[1] - 1
-    SL = 16
+    SL = 32
     lowc = lax.broadcasted_iota(jnp.int32, (KC, 128), 1) < DEPTH
 
     def multiply(jc, gp):
-        def one(g):
-            used = count[g]
-
-            def some(q, acc):
+        pair = (2 * gp, 2 * gp + 1)
+
+        def some(q, accs):
+            res = []
+            for g, acc in zip(pair, accs):
+                used = count[g]
                 parts = []
                 for p in range(SL // 2):
                     s = q * SL + 2 * p
@@ -214,11 +225,11 @@
                     parts.append(jnp.where(lowc, dup[jc, i0], dup[jc, i1]))
                 lhs = jnp.concatenate(parts, axis=1)
                 rhs = tv[g, pl.ds(pl.multiple_of(q * SL * DEPTH, SL * DEPTH), SL * DEPTH), :]
-                return acc + jnp.dot(lhs, rhs, preferred_element_type=jnp.float32)
-
-            return lax.fori_loop(0, slots // SL, some, jnp.zeros((KC, 128), jnp.float32))
-
-        a, b = one(2 * gp), one(2 * gp + 1)
+                res.append(acc + jnp.dot(lhs, rhs, preferred_element_type=jnp.float32))
+            return tuple(res)
+
+        nil = jnp.zeros((KC, 128), jnp.float32)
+        a, b = lax.fori_loop(0, slots // SL, some, (nil, nil))
         rows = pl.ds(pl.multiple_of(gp * 2 * fpd, 2 * fpd), 2 * fpd)
         for i in range(R // JC):
             both = jnp.concatenate([a[i * fpd:(i + 1) * fpd], b[i * fpd:(i + 1) * fpd]], axis=0)
@@ -248,10 +259,11 @@
         lax.fori_loop(0, R // JC, one, 0)
 
     GP = G // 2
-    first = N // JC + 2
-    rest = N + 2 - first
+    first = N // JC + LAG_C
+    rest = N + LAG_C - first
     per = max(1, rest // GP)
 
+    lax.fori_loop(0, SUB, lambda i, _: (own_out(i), 0)[1], 0)
     for g in range(G):
         tile_copy(g).start()
     lax.fori_loop(0, first, lambda n, _: (step(n), 0)[1], 0)

time: 92.9 us -> 71.2 us (0.77)
  Pallas kernels: 89.6 us -> 68 us
    pallas_call x1, Pallas kernels: 89.6 us -> 68 us  [fused(): pl.pallas_call(functools.partial(kernel, Z, W), out_shape=jax.ShapeDtypeS...]
where the time goes in v2:
time: 71.2 us; the launch traced here: 71 us
  Pallas kernels  68 us (96%)
  local copies, waits for them, and re-layouts  3.06 us (4%)
    pallas_call x1, Pallas kernels, fused(): pl.pallas_call(functools.partial(kernel, Z, W), out_shape=jax.ShapeDtypeS...  68 us
    unnamed x1, local copies, waits for them, and re-layouts  1.67 us

profile of v2, /device:TPU:25, one launch (start us, length us, event | category | flops | bytes accessed | tf_op | source)
XLA Modules:
  0.0 71.0 jit_solution(14299611837678087457)
XLA Ops:
  0.0 1.4 %copy.6.slot = s32[128,1]{1,0:T(8,128)} copy(s32[128,1]{0,1:T(1,128)} %bitcast.9) | data formatting | bytes 1024 | tf_op jit(solution)/shard_map/reshape | solution.py:355
  1.4 68.0 %shard_map.55 = bf16[16,64,128]{2,1,0:T(8,128)(2,1)} custom-call(s32[8,96]{1,0:T(8,128)} %light.1, s32[8]{0:T(128)} %count.1, s32[128,1]{1,0:T(8,128)} %copy.6.slot, bf16[1024,384]{1,0:T(8,128)(2,1)} %env.1, bf16[8,6144,128]{2,1,0:T(8,128)(2,1)} %bitcast.7), custom_call_target="tpu_custom_call" | custom-call | tf_op jit(solution)/shard_map/pallas_call | solution.py:338
  69.3 1.7 %copy.8 = bf16[8,16384]{1,0:T(8,128)(2,1)} copy(bf16[8,16384]{1,0:T(8,128)(2,1)} %bitcast.8) | data formatting | bytes 524288

commit v3 on v2

--- a/solution.py
+++ b/solution.py
@@ -12,16 +12,16 @@
 J = 4
 JC = 2
 SUB = J // JC
-LAG_B = 1
-LAG_C = 3
+LAG_B = 3
+LAG_C = 6
 MESH = pl.DeviceIdType.MESH
 
 
-def kernel(Z, W, light, count, slot, env, tiles, out,
-           own, trunk, emap, dup, tv, sb, zs, zr, fs, fr, xs, xr, ts, os_, or_):
+def kernel(Z, W, light, count, slot, env_hbm, tiles, out,
+           env, es, own, trunk, emap, dup, tv, sb, zs, zr, fs, fr, xs, xr, ts, os_, or_):
     R = 4 * Z
     G, slots = light.shape
-    L = env.shape[0]
+    L = env_hbm.shape[0]
     KJ = F // J
     KC = F // JC
     fpd = F // R
@@ -37,6 +37,8 @@
     xoff = pl.multiple_of(x * W, 128)
     xland = pl.multiple_of((1 - x) * W, 128)
 
+    load_env = pltpu.make_async_copy(env_hbm, env, es)
+    load_env.start()
     barrier = pltpu.get_barrier_semaphore()
 
     def greet(i, _):
@@ -50,6 +52,7 @@
         return pltpu.make_async_copy(tiles.at[g], tv.at[g], ts.at[g])
 
     perm = (slot[...] == lax.broadcasted_iota(jnp.int32, (F, F), 1)).astype(jnp.float32).astype(jnp.bfloat16)
+    load_env.wait()
     for c in range(CHANNELS):
         own[c] = lax.dot_general(perm, env[:, c * F:(c + 1) * F], (((1,), (1,)), ((), ())),
                                  preferred_element_type=jnp.float32).astype(jnp.bfloat16)
@@ -138,7 +141,7 @@
 
     def stage_a(j, t):
         def mine():
-            for k in (2, 3, 1, 0):
+            for k in (0, 1, 2, 3):
                 fan_copy(j, z, k, True).start()
 
         def other(zz, up):
@@ -147,7 +150,7 @@
             @pl.when(can_go(up))
             def _():
                 z_copy(j, zz, up, False).start()
-            for k in (2, 3, 1, 0):
+            for k in (0, 1, 2, 3):
                 fan_copy(j, zz, k, False).start()
 
         each_block(t, mine, other)
@@ -235,56 +238,65 @@
             both = jnp.concatenate([a[i * fpd:(i + 1) * fpd], b[i * fpd:(i + 1) * fpd]], axis=0)
             sb[jc * (R // JC) + i, rows, :] = both.astype(jnp.bfloat16)
 
-    def out_copy(d):
+    def rows_out(gp):
+        return pl.ds(pl.multiple_of(gp * 2 * fpd, 2 * fpd), 2 * fpd)
+
+    def out_copy(d, gp):
+        rows = rows_out(gp)
         return pltpu.make_async_remote_copy(
-            src_ref=sb.at[d], dst_ref=out.at[row], send_sem=os_.at[d], recv_sem=or_.at[row],
+            src_ref=sb.at[d, rows], dst_ref=out.at[row, rows], send_sem=os_.at[d, gp], recv_sem=or_.at[row, gp],
             device_id=(x, d), device_id_type=MESH)
 
-    def out_local():
-        return pltpu.make_async_copy(sb.at[row], out.at[row], or_.at[row])
-
-    def send(jc):
+    def out_local(gp):
+        rows = rows_out(gp)
+        return pltpu.make_async_copy(sb.at[row, rows], out.at[row, rows], or_.at[row, gp])
+
+    def send(jc, gp):
         def one(i, _):
             d = jc * (R // JC) + lax.rem(row + i, R // JC)
 
             @pl.when(d != row)
             def _():
-                out_copy(d).start()
+                out_copy(d, gp).start()
 
             @pl.when(d == row)
             def _():
-                out_local().start()
+                out_local(gp).start()
             return 0
 
         lax.fori_loop(0, R // JC, one, 0)
 
     GP = G // 2
     first = N // JC + LAG_C
-    rest = N + LAG_C - first
+    rest = N + LAG_C - max(first, G)
     per = max(1, rest // GP)
 
     lax.fori_loop(0, SUB, lambda i, _: (own_out(i), 0)[1], 0)
-    for g in range(G):
-        tile_copy(g).start()
-    lax.fori_loop(0, first, lambda n, _: (step(n), 0)[1], 0)
+
+    def begin(n, _):
+        step(n)
+
+        @pl.when(n < G)
+        def _():
+            tile_copy(n).start()
+        return 0
+
+    lax.fori_loop(0, max(first, G), begin, 0)
     for g in range(G):
         tile_copy(g).wait()
 
     def second(i, _):
-        step(first + i)
+        step(max(first, G) + i)
 
         @pl.when((lax.rem(i, per) == 0) & (lax.div(i, per) < GP))
         def _():
             multiply(0, lax.div(i, per))
-
-        @pl.when(i == (GP - 1) * per)
-        def _():
-            send(0)
+            send(0, lax.div(i, per))
+
         return 0
 
     lax.fori_loop(0, rest, second, 0)
-    lax.fori_loop(0, GP, lambda gp, _: (multiply(1, gp), 0)[1], 0)
-    send(1)
+    lax.fori_loop(0, GP, lambda gp, _: (multiply(1, gp), send(1, gp), 0)[2], 0)
 
     def drain(n, _):
         j, t = lax.div(n, Z), lax.rem(n, Z)
@@ -310,20 +322,23 @@
 
     lax.fori_loop(0, N, drain, 0)
 
-    def finish(d, _):
+    def finish(n, _):
+        d, gp = lax.div(n, GP), lax.rem(n, GP)
+
         @pl.when(d != row)
         def _():
-            out_copy(d).wait_send()
+            out_copy(d, gp).wait_send()
+            here = out.at[d, rows_out(gp)]
             pltpu.make_async_remote_copy(
-                src_ref=out.at[d], dst_ref=out.at[d], send_sem=os_.at[d], recv_sem=or_.at[d],
+                src_ref=here, dst_ref=here, send_sem=os_.at[d, gp], recv_sem=or_.at[d, gp],
                 device_id=(x, d), device_id_type=MESH).wait_recv()
 
         @pl.when(d == row)
         def _():
-            out_local().wait()
+            out_local(gp).wait()
         return 0
 
-    lax.fori_loop(0, R, finish, 0)
+    lax.fori_loop(0, R * GP, finish, 0)
 
 
 def fused(Z, W, tiles, tile_light, tile_count, env_maps, frame_slot):
@@ -334,13 +349,15 @@
     bf = jnp.bfloat16
     dma = pltpu.SemaphoreType.DMA
     vmem = pl.BlockSpec(memory_space=pltpu.VMEM)
+    hbm = pl.BlockSpec(memory_space=pl.ANY)
     smem = pl.BlockSpec(memory_space=pltpu.SMEM)
     pieces = pl.pallas_call(
         functools.partial(kernel, Z, W),
         out_shape=jax.ShapeDtypeStruct((R, G * fpd, width), bf),
-        in_specs=[smem, smem, vmem, vmem, pl.BlockSpec(memory_space=pl.ANY)],
+        in_specs=[smem, smem, vmem, hbm, hbm],
         out_specs=vmem,
         scratch_shapes=[
+            pltpu.VMEM(env_maps.shape, bf), dma(()),
             pltpu.VMEM((CHANNELS, F, L), bf),
             pltpu.VMEM((Z, CHANNELS, F, W), bf),
             pltpu.VMEM((Z, 4, F, L), bf),
@@ -348,7 +365,7 @@
             pltpu.VMEM((G, slots * depth, width), bf),
             pltpu.VMEM((R, G * fpd, width), bf),
             dma((J, 2, Z)), dma((J, Z)), dma((J, Z, 4)), dma((J, Z, 4)),
-            dma((J, Z)), dma((J, Z)), dma((G,)), dma((R,)), dma((R,)),
+            dma((J, Z)), dma((J, Z)), dma((G,)), dma((R, G // 2)), dma((R, G // 2)),
         ],
         compiler_params=pltpu.CompilerParams(
             collective_id=0, has_side_effects=True, vmem_limit_bytes=56 * 1024 * 1024),

time: 71.2 us -> 66.5 us (0.934)
  Pallas kernels: 68 us -> 62.8 us
    pallas_call x1, Pallas kernels: 68 us -> 62.8 us  [fused(): pl.pallas_call(functools.partial(kernel, Z, W), out_shape=jax.ShapeDtypeS...]
where the time goes in v3:
time: 66.5 us; the launch traced here: 65.9 us
  Pallas kernels  62.8 us (94%)
  local copies, waits for them, and re-layouts  3.06 us (5%)
    pallas_call x1, Pallas kernels, fused(): pl.pallas_call(functools.partial(kernel, Z, W), out_shape=jax.ShapeDtypeS...  62.8 us
    unnamed x1, local copies, waits for them, and re-layouts  1.67 us
    reshape x1, local copies, waits for them, and re-layouts, fused(): frame_slot.reshape(F, 1)  1.39 us

profile of v3, /device:TPU:25, one launch (start us, length us, event | category | flops | bytes accessed | tf_op | source)
XLA Modules:
  0.0 65.9 jit_solution(9769761878526645054)
XLA Ops:
  0.0 1.4 %copy.6.slot = s32[128,1]{1,0:T(8,128)} copy(s32[128,1]{0,1:T(1,128)} %bitcast.9) | data formatting | bytes 1024 | tf_op jit(solution)/shard_map/reshape | solution.py:372
  1.4 62.8 %shard_map.55 = bf16[16,64,128]{2,1,0:T(8,128)(2,1)} custom-call(s32[8,96]{1,0:T(8,128)} %light.1, s32[8]{0:T(128)} %count.1, s32[128,1]{1,0:T(8,128)} %copy.6.slot, bf16[1024,384]{1,0:T(8,128)(2,1)} %env_hbm.1, bf16[8,6144,128]{2,1,0:T(8,128)(2,1)} %bitcast.7), custom_call_target="tpu_custom_call" | custom-call | tf_op jit(solution)/shard_map/pallas_call | solution.py:354
  64.2 1.7 %copy.8 = bf16[8,16384]{1,0:T(8,128)(2,1)} copy(bf16[8,16384]{1,0:T(8,128)(2,1)} %bitcast.8) | data formatting | bytes 524288
